TPU v7x, 256 devices: a whole 4x4x8 slice. The times are simulated.
256 devices in a mesh: feat: 64 (over x, z_lo, y), dp: 4 (over z_hi, core).
Axes of the slice: x: 4, y: 4, z: 8 (z_hi: 2, z_lo: 4; z = z_hi * 4 + z_lo), core: 2. Of those that a mesh axis runs over, the one named last changes fastest.
Arguments:
- inputs: bfloat16 [1024, 65536], P('dp', 'feat'), may hold values from -6 to 6
- weights: bfloat16 [128, 8, 512, 512], P('feat'), may hold values from -0.09375 to 0.09375
- cotangent: bfloat16 [1024, 65536], P('dp', 'feat'), may hold values from -0.75 to 0.75
Outputs:
- outputs: bfloat16 [1024, 65536], P('dp', 'feat')
- input_grad: bfloat16 [1024, 65536], P('dp', 'feat')
- weight_grad: bfloat16 [128, 8, 512, 512], P('feat', None, 'dp')
All inputs are finite; a program needn't handle non-finite values.
Results may differ from a plain program's by a relative error of at most 0.0047.
Values may be sent and summed in bfloat16 or wider, within the bound.
A program may use at most 128 MiB of HBM per device.

v0:
```python
import jax
import jax.numpy as jnp
from jax import lax
from jax.sharding import PartitionSpec as P


def partner(value, axis, distance):
    mask = 2**distance
    pairs = [(source, source ^ mask) for source in range(lax.axis_size(axis))]
    return lax.ppermute(value, axis, pairs)


def flip_rows(values, bit_level):
    row_count, tokens, last_size = values.shape
    halves = values.reshape(row_count >> bit_level + 1, 2, 1 << bit_level, tokens, last_size)
    return jnp.flip(halves, 1).reshape(row_count, tokens, last_size)


def body(inputs, weights, cotangent):
    row_count = weights.shape[0]
    slot_count = weights.shape[1]
    block_size = weights.shape[2]
    levels = slot_count - 1
    tokens = inputs.shape[0]
    local_bits = row_count.bit_length() - 1
    features = jnp.transpose(inputs.reshape(tokens, row_count, block_size), (1, 0, 2))
    upstream = jnp.transpose(cotangent.reshape(tokens, row_count, block_size), (1, 0, 2))
    visit_list = list(range(levels))
    partner_rows = {}
    for bit_level in visit_list:
        if bit_level < local_bits:
            partner_rows[bit_level] = flip_rows(features, bit_level)
        else:
            partner_rows[bit_level] = partner(features, "feat", bit_level - local_bits)
    forward_stack = jnp.stack([features] + [partner_rows[level] for level in range(levels)], axis=1)
    summed = jnp.einsum(
        "rsta,rsab->rtb", forward_stack, weights, preferred_element_type=jnp.float32
    )
    outputs = jnp.transpose(summed.astype(jnp.bfloat16), (1, 0, 2)).reshape(
        tokens, row_count * block_size
    )
    back_terms = jnp.einsum("rtb,rsab->rsta", upstream, weights, preferred_element_type=jnp.float32)
    grad_total = back_terms[:, 0]
    rounded_terms = back_terms[:, 1:].astype(jnp.bfloat16)
    for bit_level in range(levels):
        partial_term = rounded_terms[:, bit_level]
        if bit_level < local_bits:
            arrived = flip_rows(partial_term, bit_level)
        else:
            arrived = partner(partial_term, "feat", bit_level - local_bits)
        grad_total = grad_total + arrived.astype(jnp.float32)
    input_grad = jnp.transpose(grad_total.astype(jnp.bfloat16), (1, 0, 2)).reshape(
        tokens, row_count * block_size
    )
    columns = lax.all_to_all(forward_stack, "dp", split_axis=3, concat_axis=2, tiled=True)
    weight_sum = jnp.einsum(
        "rsta,rtb->rsab",
        columns,
        lax.all_gather(upstream, "dp", axis=1, tiled=True),
        preferred_element_type=jnp.float32,
    )
    weight_grad = weight_sum.astype(jnp.bfloat16)
    return (outputs, input_grad, weight_grad)


def solution(mesh):
    in_specs = (P("dp", "feat"), P("feat", None, None, None), P("dp", "feat"))
    out_specs = (P("dp", "feat"), P("dp", "feat"), P("feat", None, "dp", None))
    return jax.shard_map(body, mesh=mesh, in_specs=in_specs, out_specs=out_specs, check_vma=False)
```

profile of v0, /device:TPU:1, one launch (start us, length us, event | category | flops | bytes accessed | tf_op | source)
XLA Modules:
  0.0 235.6 jit_solution(11875098161094299809)
XLA Ops:
  7.2 1.2 copy.44
  8.4 0.2 copy.45
  8.6 2.2 collective-permute-start
  10.8 2.6 %collective-permute-start.1 = (bf16[2,256,512]{2,1,0:T(8,128)(2,1)S(1)}, bf16[2,256,512]{2,1,0:T(8,128)(2,1)S(1)}, u32[]{:S(2)}, u32[]{:S(2)}) collective-permute-start(bf16[2,256,512]{2,1,0:T(8,128)(2,1)S(1)} %bitcast.137), channel_id=1, source_target_pairs={{0,8},{4,12},{8,0},{12,4},{16,24},{20,28},{24,16},{28,20},{32,40},... | collective-permute-start | bytes 1572872 | tf_op jit(solution)/shard_map/ppermute | solution.py:10
  13.5 1.6 collective-permute-start.2
  15.1 3.0 %collective-permute-start.3 = (bf16[2,256,512]{2,1,0:T(8,128)(2,1)S(1)}, bf16[2,256,512]{2,1,0:T(8,128)(2,1)S(1)}, u32[]{:S(2)}, u32[]{:S(2)}) collective-permute-start(bf16[2,256,512]{2,1,0:T(8,128)(2,1)S(1)} %bitcast.139), channel_id=1, source_target_pairs={{0,32},{4,36},{8,40},{12,44},{16,48},{20,52},{24,56},{28,60},{32,0... | collective-permute-start | bytes 1572872 | tf_op jit(solution)/shard_map/ppermute | solution.py:10
  18.1 1.2 collective-permute-start.4
  19.3 0.8 bitcast_dynamic-update-slice_fusion.6
  20.1 0.9 bitcast_dynamic-update-slice_fusion.5
  21.0 0.2 collective-permute-done
  21.2 3.8 %collective-permute-start.5 = (bf16[2,256,512]{2,1,0:T(8,128)(2,1)S(1)}, bf16[2,256,512]{2,1,0:T(8,128)(2,1)S(1)}, u32[]{:S(2)}, u32[]{:S(2)}) collective-permute-start(bf16[2,256,512]{2,1,0:T(8,128)(2,1)S(1)} %bitcast.142), channel_id=1, source_target_pairs={{0,128},{4,132},{8,136},{12,140},{16,144},{20,148},{24,152},{28,15... | collective-permute-start | bytes 1572872 | tf_op jit(solution)/shard_map/ppermute | solution.py:10
  25.1 0.9 bitcast_dynamic-update-slice_fusion.4
  25.9 10.1 %collective-permute-done.1 = bf16[2,256,512]{2,1,0:T(8,128)(2,1)S(1)} collective-permute-done((bf16[2,256,512]{2,1,0:T(8,128)(2,1)S(1)}, bf16[2,256,512]{2,1,0:T(8,128)(2,1)S(1)}, u32[]{:S(2)}, u32[]{:S(2)}) %collective-permute-start.1) | collective-permute-done | bytes 524320 | tf_op jit(solution)/shard_map/ppermute | solution.py:10
  36.0 0.8 bitcast_dynamic-update-slice_fusion.3
  36.8 0.1 collective-permute-done.2
  37.0 0.8 bitcast_dynamic-update-slice_fusion.2
  37.8 0.0 collective-permute-done.3
  37.8 0.8 bitcast_dynamic-update-slice_fusion.1
  38.7 0.0 collective-permute-done.4
  38.7 0.8 bitcast_dynamic-update-slice_fusion
  39.5 3.7 %collective-permute-done.5 = bf16[2,256,512]{2,1,0:T(8,128)(2,1)S(1)} collective-permute-done((bf16[2,256,512]{2,1,0:T(8,128)(2,1)S(1)}, bf16[2,256,512]{2,1,0:T(8,128)(2,1)S(1)}, u32[]{:S(2)}, u32[]{:S(2)}) %collective-permute-start.5) | collective-permute-done | bytes 524320 | tf_op jit(solution)/shard_map/ppermute | solution.py:10
  43.1 0.8 bitcast_dynamic-update-slice_fusion.7
  44.0 7.9 %copy.63 = bf16[2,8,256,512]{2,1,0,3:T(8,128)(2,1)} copy(bf16[2,8,256,512]{3,2,1,0:T(8,128)(2,1)} %bitcast_dynamic-update-slice_fusion.7) | data formatting | bytes 8388608 | tf_op jit(solution)/shard_map/stack | solution.py:35
  51.9 8.6 %all-to-all-start = ((bf16[2,8,256,512]{2,1,0,3:T(8,128)(2,1)}), bf16[2,8,256,512]{2,1,0,3:T(8,128)(2,1)}, u32[]{:S(2)}, u32[]{:S(2)}) async-start(bf16[2,8,256,512]{2,1,0,3:T(8,128)(2,1)} %copy.63), calls=%async_computation | async-start | bytes 8388608 | tf_op jit(solution)/shard_map/all_to_all | solution.py:55
  60.5 0.2 copy.54
  60.7 1.0 copy.55
  61.7 0.0 all-gather.2.cloned.1.call-update
  61.7 5.8 %fusion.17 = (bf16[2,8,256,512]{2,3,1,0:T(8,128)(2,1)S(1)}, f32[2,8,256,512]{2,3,1,0:T(8,128)S(1)}) fusion(bf16[2,8,512,512]{3,2,1,0:T(8,128)(2,1)} %param.4, bf16[256,2,512]{2,0,1:T(8,128)(2,1)} %copy.55), kind=kOutput, calls=%fused_computation.34 | convolution fusion | flops 2149580800 | bytes 21495808 | tf_op jit(solution)/shard_map/rtb,rsab->rsta/dot_general | solution.py:42
  67.6 0.3 slice_bitcast_fusion.7
  67.8 0.5 collective-permute-start.10
  68.3 2.4 %collective-permute-start.11 = (bf16[2,256,512]{1,2,0:T(8,128)(2,1)S(1)}, bf16[2,256,512]{1,2,0:T(8,128)(2,1)S(1)}, u32[]{:S(2)}, u32[]{:S(2)}) collective-permute-start(bf16[2,256,512]{1,2,0:T(8,128)(2,1)S(1)} %get-tuple-element.17), channel_id=1, source_target_pairs={{0,128},{4,132},{8,136},{12,140},{16,144},{20,148},{24,152},{28,15... | collective-permute-start | bytes 1572872 | tf_op jit(solution)/shard_map/ppermute | solution.py:10
  70.8 0.0 collective-permute-start.6
  70.8 1.1 collective-permute-start.7
  71.9 9.7 %collective-permute-done.10 = bf16[2,256,512]{1,2,0:T(8,128)(2,1)S(1)} collective-permute-done((bf16[2,256,512]{1,2,0:T(8,128)(2,1)S(1)}, bf16[2,256,512]{1,2,0:T(8,128)(2,1)S(1)}, u32[]{:S(2)}, u32[]{:S(2)}) %collective-permute-start.10) | collective-permute-done | bytes 524320 | tf_op jit(solution)/shard_map/ppermute | solution.py:10
  81.6 1.2 collective-permute-start.9
  82.7 11.5 %collective-permute-done.11 = bf16[2,256,512]{1,2,0:T(8,128)(2,1)S(1)} collective-permute-done((bf16[2,256,512]{1,2,0:T(8,128)(2,1)S(1)}, bf16[2,256,512]{1,2,0:T(8,128)(2,1)S(1)}, u32[]{:S(2)}, u32[]{:S(2)}) %collective-permute-start.11) | collective-permute-done | bytes 524320 | tf_op jit(solution)/shard_map/ppermute | solution.py:10
  94.2 0.0 collective-permute-done.6
  94.2 0.5 collective-permute-done.7
  94.7 102.5 %collective-permute-done.8 = bf16[2,256,512]{1,2,0:T(8,128)(2,1)S(1)} collective-permute-done((bf16[2,256,512]{1,2,0:T(8,128)(2,1)S(1)}, bf16[2,256,512]{1,2,0:T(8,128)(2,1)S(1)}, u32[]{:S(2)}, u32[]{:S(2)}) %collective-permute-start.8) | collective-permute-done | bytes 524320 | tf_op jit(solution)/shard_map/ppermute | solution.py:10
  197.2 0.0 collective-permute-done.9
  197.3 0.6 fusion.15
  197.8 1.0 copy.66
  198.9 7.0 %fusion.6 = bf16[256,2,512]{2,0,1:T(8,128)(2,1)S(1)} fusion(bf16[2,8,256,512]{3,2,1,0:T(8,128)(2,1)} %bitcast_dynamic-update-slice_fusion.7, bf16[2,8,512,512]{3,2,1,0:T(8,128)(2,1)} %param.4), kind=kOutput, calls=%fused_computation.7 | convolution fusion | flops 2147745792 | bytes 13107200 | tf_op jit(solution)/shard_map/rsta,rsab->rtb/dot_general | solution.py:36
  205.8 0.2 copy.53
  206.0 1.0 copy.65
  207.1 7.4 %copy.78 = bf16[2,8,256,4,128]{2,3,4,1,0:T(4,128)(2,1)} copy(bf16[2,8,256,4,128]{2,1,0,4,3:T(8,128)(2,1)} %bitcast.35) | data formatting | bytes 8388608 | tf_op jit(solution)/shard_map/all_to_all | solution.py:55
  214.5 7.7 %all_to_all.16 = bf16[2,8,1024,128]{2,3,1,0:T(8,128)(2,1)} reshape(bf16[2,8,4,256,128]{3,2,4,1,0:T(4,128)(2,1)} %bitcast.135) | data formatting | bytes 8388608 | tf_op jit(solution)/shard_map/all_to_all | solution.py:55
  222.2 6.5 %fusion.2 = bf16[2,8,128,512]{3,2,1,0:T(8,128)(2,1)} fusion(bf16[2,8,1024,128]{2,3,1,0:T(8,128)(2,1)} %all_to_all.16, bf16[2,1024,512]{2,1,0:T(8,128)(2,1)} %all-gather.2.cloned.1.call-done), kind=kOutput, calls=%fused_computation.4 | convolution fusion | flops 2148532224 | bytes 8388608 | tf_op jit(solution)/shard_map/rsta,rtb->rsab/dot_general | solution.py:56
  (6 shorter events, 0.0 us)
Async XLA Ops:
  8.6 12.6 %collective-permute-start = (bf16[2,256,512]{2,1,0:T(8,128)(2,1)S(1)}, bf16[2,256,512]{2,1,0:T(8,128)(2,1)S(1)}, u32[]{:S(2)}, u32[]{:S(2)}) collective-permute-start(bf16[2,256,512]{2,1,0:T(8,128)(2,1)S(1)} %bitcast.136), channel_id=1, source_target_pairs={{0,4},{4,0},{8,12},{12,8},{16,20},{20,16},{24,28},{28,24},{32,36},... | collective-permute-start | bytes 1572872 | tf_op jit(solution)/shard_map/ppermute | solution.py:10
  10.8 25.2 %collective-permute-start.1 = (bf16[2,256,512]{2,1,0:T(8,128)(2,1)S(1)}, bf16[2,256,512]{2,1,0:T(8,128)(2,1)S(1)}, u32[]{:S(2)}, u32[]{:S(2)}) collective-permute-start(bf16[2,256,512]{2,1,0:T(8,128)(2,1)S(1)} %bitcast.137), channel_id=1, source_target_pairs={{0,8},{4,12},{8,0},{12,4},{16,24},{20,28},{24,16},{28,20},{32,40},... | collective-permute-start | bytes 1572872 | tf_op jit(solution)/shard_map/ppermute | solution.py:10
  13.5 23.5 %collective-permute-start.2 = (bf16[2,256,512]{2,1,0:T(8,128)(2,1)S(1)}, bf16[2,256,512]{2,1,0:T(8,128)(2,1)S(1)}, u32[]{:S(2)}, u32[]{:S(2)}) collective-permute-start(bf16[2,256,512]{2,1,0:T(8,128)(2,1)S(1)} %bitcast.138), channel_id=1, source_target_pairs={{0,16},{4,20},{8,24},{12,28},{16,0},{20,4},{24,8},{28,12},{32,48},... | collective-permute-start | bytes 1572872 | tf_op jit(solution)/shard_map/ppermute | solution.py:10
  15.1 22.7 %collective-permute-start.3 = (bf16[2,256,512]{2,1,0:T(8,128)(2,1)S(1)}, bf16[2,256,512]{2,1,0:T(8,128)(2,1)S(1)}, u32[]{:S(2)}, u32[]{:S(2)}) collective-permute-start(bf16[2,256,512]{2,1,0:T(8,128)(2,1)S(1)} %bitcast.139), channel_id=1, source_target_pairs={{0,32},{4,36},{8,40},{12,44},{16,48},{20,52},{24,56},{28,60},{32,0... | collective-permute-start | bytes 1572872 | tf_op jit(solution)/shard_map/ppermute | solution.py:10
  18.1 20.6 %collective-permute-start.4 = (bf16[2,256,512]{2,1,0:T(8,128)(2,1)S(1)}, bf16[2,256,512]{2,1,0:T(8,128)(2,1)S(1)}, u32[]{:S(2)}, u32[]{:S(2)}) collective-permute-start(bf16[2,256,512]{2,1,0:T(8,128)(2,1)S(1)} %bitcast.140), channel_id=1, source_target_pairs={{0,64},{4,68},{8,72},{12,76},{16,80},{20,84},{24,88},{28,92},{32,9... | collective-permute-start | bytes 1572872 | tf_op jit(solution)/shard_map/ppermute | solution.py:10
  21.2 21.9 %collective-permute-start.5 = (bf16[2,256,512]{2,1,0:T(8,128)(2,1)S(1)}, bf16[2,256,512]{2,1,0:T(8,128)(2,1)S(1)}, u32[]{:S(2)}, u32[]{:S(2)}) collective-permute-start(bf16[2,256,512]{2,1,0:T(8,128)(2,1)S(1)} %bitcast.142), channel_id=1, source_target_pairs={{0,128},{4,132},{8,136},{12,140},{16,144},{20,148},{24,152},{28,15... | collective-permute-start | bytes 1572872 | tf_op jit(solution)/shard_map/ppermute | solution.py:10
  51.9 8.6 %copy-start = (bf16[256,1024]{1,0:T(8,128)(2,1)S(1)}, bf16[256,1024]{1,0:T(8,128)(2,1)}, u32[]{:S(2)}) copy-start(bf16[256,1024]{1,0:T(8,128)(2,1)} %param.5) | copy-start | bytes 1572868
  51.9 155.2 %all-to-all-start = ((bf16[2,8,256,512]{2,1,0,3:T(8,128)(2,1)}), bf16[2,8,256,512]{2,1,0,3:T(8,128)(2,1)}, u32[]{:S(2)}, u32[]{:S(2)}) async-start(bf16[2,8,256,512]{2,1,0,3:T(8,128)(2,1)} %copy.63), calls=%async_computation | async-start | bytes 8388608 | tf_op jit(solution)/shard_map/all_to_all | solution.py:55
  60.5 161.7 %all-gather.2.cloned.1.call-start = ((), (), s32[]{:S(2)}) async-start(), calls=%async_computation.1 | async-start | bytes 2621440 | tf_op jit(solution)/shard_map/all_gather | solution.py:59
  67.8 13.7 %collective-permute-start.10 = (bf16[2,256,512]{1,2,0:T(8,128)(2,1)S(1)}, bf16[2,256,512]{1,2,0:T(8,128)(2,1)S(1)}, u32[]{:S(2)}, u32[]{:S(2)}) collective-permute-start(bf16[2,256,512]{1,2,0:T(8,128)(2,1)S(1)} %get-tuple-element.18), channel_id=1, source_target_pairs={{0,64},{4,68},{8,72},{12,76},{16,80},{20,84},{24,88},{28,92},{32,9... | collective-permute-start | bytes 1572872 | tf_op jit(solution)/shard_map/ppermute | solution.py:10
  68.3 25.9 %collective-permute-start.11 = (bf16[2,256,512]{1,2,0:T(8,128)(2,1)S(1)}, bf16[2,256,512]{1,2,0:T(8,128)(2,1)S(1)}, u32[]{:S(2)}, u32[]{:S(2)}) collective-permute-start(bf16[2,256,512]{1,2,0:T(8,128)(2,1)S(1)} %get-tuple-element.17), channel_id=1, source_target_pairs={{0,128},{4,132},{8,136},{12,140},{16,144},{20,148},{24,152},{28,15... | collective-permute-start | bytes 1572872 | tf_op jit(solution)/shard_map/ppermute | solution.py:10
  70.8 23.4 %collective-permute-start.6 = (bf16[2,256,512]{1,2,0:T(8,128)(2,1)S(1)}, bf16[2,256,512]{1,2,0:T(8,128)(2,1)S(1)}, u32[]{:S(2)}, u32[]{:S(2)}) collective-permute-start(bf16[2,256,512]{1,2,0:T(8,128)(2,1)S(1)} %get-tuple-element.16), channel_id=1, source_target_pairs={{0,4},{4,0},{8,12},{12,8},{16,20},{20,16},{24,28},{28,24},{32,36},... | collective-permute-start | bytes 1572872 | tf_op jit(solution)/shard_map/ppermute | solution.py:10
  70.8 23.9 %collective-permute-start.7 = (bf16[2,256,512]{1,2,0:T(8,128)(2,1)S(1)}, bf16[2,256,512]{1,2,0:T(8,128)(2,1)S(1)}, u32[]{:S(2)}, u32[]{:S(2)}) collective-permute-start(bf16[2,256,512]{1,2,0:T(8,128)(2,1)S(1)} %get-tuple-element.15), channel_id=1, source_target_pairs={{0,8},{4,12},{8,0},{12,4},{16,24},{20,28},{24,16},{28,20},{32,40},... | collective-permute-start | bytes 1572872 | tf_op jit(solution)/shard_map/ppermute | solution.py:10
  71.9 125.3 %collective-permute-start.8 = (bf16[2,256,512]{1,2,0:T(8,128)(2,1)S(1)}, bf16[2,256,512]{1,2,0:T(8,128)(2,1)S(1)}, u32[]{:S(2)}, u32[]{:S(2)}) collective-permute-start(bf16[2,256,512]{1,2,0:T(8,128)(2,1)S(1)} %get-tuple-element.14), channel_id=1, source_target_pairs={{0,16},{4,20},{8,24},{12,28},{16,0},{20,4},{24,8},{28,12},{32,48},... | collective-permute-start | bytes 1572872 | tf_op jit(solution)/shard_map/ppermute | solution.py:10
  81.6 115.7 %collective-permute-start.9 = (bf16[2,256,512]{1,2,0:T(8,128)(2,1)S(1)}, bf16[2,256,512]{1,2,0:T(8,128)(2,1)S(1)}, u32[]{:S(2)}, u32[]{:S(2)}) collective-permute-start(bf16[2,256,512]{1,2,0:T(8,128)(2,1)S(1)} %get-tuple-element.13), channel_id=1, source_target_pairs={{0,32},{4,36},{8,40},{12,44},{16,48},{20,52},{24,56},{28,60},{32,0... | collective-permute-start | bytes 1572872 | tf_op jit(solution)/shard_map/ppermute | solution.py:10
Sparse Core Ops, SparseCore 0:
  63.7 50.5 all-gather.1
where the time goes:
time: 236 us
  waiting for transfers between devices  138 us (58%)
  local copies, waits for them, and re-layouts  34.9 us (15%)
  starting transfers between devices  28.4 us (12%)
  matrix products  19.3 us (8%)
  between operations  14.1 us (6%)
    ppermute x12, waiting for transfers between devices, partner(): return lax.ppermute(value, axis, pairs)  138 us
    ppermute x12, starting transfers between devices, partner(): return lax.ppermute(value, axis, pairs)  19.8 us
    all_to_all x2, local copies, waits for them, and re-layouts, body(): lax.all_to_all(forward_stack, 'dp', split_axis=3, concat_axis=2, tiled=True)  15.1 us
    unnamed x14, local copies, waits for them, and re-layouts  9.61 us
    another operation x2, local copies, waits for them, and re-layouts, body(): jnp.stack([features] + [partner_rows[level] for level in range(levels)],...  8.75 us
    all_to_all x1, starting transfers between devices, body(): lax.all_to_all(forward_stack, 'dp', split_axis=3, concat_axis=2, tiled=True)  8.61 us
    dot_general x1, matrix products, body(): jnp.einsum('rsta,rsab->rtb', forward_stack, weights, preferred_element_ty...  6.98 us
    dot_general x1, matrix products, body(): jnp.einsum('rsta,rtb->rsab', columns, lax.all_gather(upstream, 'dp', axis...  6.54 us
  transfers between devices with their start and end apart: 14, of which 8 were waited for; matrix products, arithmetic and copies ran while one was open for 13% of the time, Pallas kernels for 0%

commit v1 on v0

v1 whole, which is shorter than its diff:
```python
import jax
import jax.numpy as jnp
from jax import lax
from jax.experimental import pallas as pl
from jax.experimental.pallas import tpu as pltpu
from jax.sharding import PartitionSpec as P

MESH = pl.DeviceIdType.MESH
BF16 = jnp.bfloat16
F32 = jnp.float32
OTHER = 16
NAMES = (
    ["S1", "S2", "L2", "L3", "L4", "G", "A1", "A2"]
    + ["Y1", "Y2", "X1", "X2", "OY1", "OY2", "OX1", "OX2"]
    + ["B2", "B3", "B6", "B7", "R0", "R1", "Q0", "Q1", "CG", "CH"]
    + [f"C{s}" for s in (0, 2, 3, 4, 5, 6, 7)]
    + [f"D{s}" for s in (0, 2, 3, 4, 5, 6, 7)]
)
IDS = {name: number for number, name in enumerate(NAMES)}
TERM = {2: 0, 3: 1, 6: 2, 7: 3, 5: 4, 4: 5}


def kernel(x_ref, w_ref, g_ref, out_ref, ig_ref, dw_ref, xb, sx, wb, gb, rb, sb, acc_o, acc_g, ob, db,
           send_sem, recv_sem, x_sem, g_sem, w_sem, o_sem):
    feat = lax.axis_index("feat")
    dp = lax.axis_index("dp")
    y = feat % 4
    z_lo = (feat // 4) % 4
    x = feat // 16
    side = dp // 2
    core = dp % 2
    z = side * 4 + z_lo
    ey = 1 - 2 * (y % 2)
    ex = 1 - 2 * (x % 2)
    ez = 1 - 2 * (z % 2)
    middle = ((z_lo + 1) // 2) % 2
    end = 1 - middle
    away = 1 - side

    def at_y(step):
        return (x * 16 + z_lo * 4 + (y + step + 4) % 4, dp)

    def at_x(step):
        return (((x + step + 4) % 4) * 16 + z_lo * 4 + y, dp)

    def at_z(step):
        there = (z + step + 8) % 8
        return (x * 16 + (there % 4) * 4 + y, (there // 4) * 2 + core)

    sibling = (feat, side * 2 + 1 - core)
    z_first = at_z(ez)
    z_second = (x * 16 + ((z_lo + 2) % 4) * 4 + y, dp)
    second = end * (OTHER + 5) + middle * (10 + away)

    loads = []
    for d in range(4):
        for r in range(2):
            load = pltpu.make_async_copy(
                x_ref.at[:, pl.ds(r * 512 + d * 128, 128)], xb.at[d // 2, d % 2, r], x_sem.at[d * 2 + r]
            )
            load.start()
            loads.append(load)
    g_loads = []
    for r in range(2):
        load = pltpu.make_async_copy(g_ref.at[:, pl.ds(r * 512, 512)], gb.at[r, 0], g_sem.at[r])
        load.start()
        g_loads.append(load)
    w_loads = {}
    for s in (3, 7, 2, 6, 0, 1, 4, 5):
        w_loads[s] = pltpu.make_async_copy(w_ref.at[:, s], wb.at[s], w_sem.at[s])
        w_loads[s].start()

    barrier = pltpu.get_barrier_semaphore()
    friends = [sibling, at_z(1), at_z(-1), at_z(2), at_z(-2), at_z(4), at_y(1), at_y(-1), at_y(2), at_x(1), at_x(-1), at_x(2)]
    for friend in friends:
        pl.semaphore_signal(barrier, inc=1, device_id=friend, device_id_type=MESH)
    pl.semaphore_wait(barrier, len(friends))

    copies = {}

    def send(name, src, dst, device):
        copies[name] = pltpu.make_async_remote_copy(
            src_ref=src, dst_ref=dst, send_sem=send_sem.at[IDS[name]], recv_sem=recv_sem.at[IDS[name]],
            device_id=device, device_id_type=MESH,
        )
        copies[name].start()

    def arrived(name):
        copies[name].wait_recv()

    def share_same(s):
        send(f"C{s}", xb.at[2 * s + side, 1 - core], sx.at[s, 0], sibling)

    def share_other(s):
        send(f"D{s}", xb.at[OTHER + s, 1 - core], sx.at[s, 1], sibling)

    def forward(s, start=False):
        base = 0 if s == 1 else 2 * s

        def row(r, carry):
            k = 1 - r if s == 1 else r
            block = jnp.concatenate([xb[base + d // 2, d % 2, k] for d in range(4)], axis=1)
            part = jnp.dot(block, wb[s, r], preferred_element_type=F32)
            if start:
                acc_o[r] = part
            else:
                acc_o[r] += part
            return carry

        lax.fori_loop(0, 2, row, 0)

    def term(s, r, q=0):
        return lax.dot_general(gb[r, q], wb[s, r], (((1,), (1,)), ((), ())), preferred_element_type=F32)

    def back(s):
        def row(r, carry):
            sb[TERM[s], r] = term(s, r).astype(BF16)
            return carry

        lax.fori_loop(0, 2, row, 0)

    def back_local():
        def row(r, carry):
            acc_g[r] = term(0, r) + term(1, 1 - r).astype(BF16).astype(F32)
            return carry

        lax.fori_loop(0, 2, row, 0)

    def add_terms(k):
        def row(r, carry):
            acc_g[r] += rb[k, r].astype(F32)
            return carry

        lax.fori_loop(0, 2, row, 0)

    stores = []

    def weight_grad(s):
        base = 0 if s == 1 else s

        def row(r, carry):
            k = 1 - r if s == 1 else r
            tokens = jnp.concatenate(
                [xb[2 * base + side, core, k], sx[base, 0, k], xb[OTHER + base, core, k], sx[base, 1, k]], axis=0
            )
            total = lax.dot_general(
                tokens, gb[r].reshape(1024, 512), (((0,), (0,)), ((), ())), preferred_element_type=F32
            )
            db[s, r] = total.astype(BF16)
            return carry

        lax.fori_loop(0, 2, row, 0)
        store = pltpu.make_async_copy(db.at[s], dw_ref.at[:, s], o_sem.at[4 + s])
        store.start()
        stores.append(store)

    for load in loads:
        load.wait()
    send("S1", xb.at[away], xb.at[8 + away], z_first)
    send("L2", xb.at[away], xb.at[second], at_z(-2 * ez))
    send("Y1", xb.at[pl.ds(0, 2)], xb.at[pl.ds(4, 2)], at_y(ey))
    send("X1", xb.at[pl.ds(0, 2)], xb.at[pl.ds(12, 2)], at_x(ex))
    for load in g_loads:
        load.wait()
    send("G", gb.at[:, 0], gb.at[:, 2], at_z(4))
    share_same(0)
    send("CG", gb.at[:, 0], gb.at[:, 1], sibling)

    for s, device in ((3, at_y(2)), (7, at_x(2)), (2, at_y(ey)), (6, at_x(ex))):
        w_loads[s].wait()
        back(s)
        send(f"B{s}", sb.at[TERM[s]], rb.at[TERM[s]], device)
    w_loads[0].wait()
    w_loads[1].wait()
    forward(0, start=True)
    forward(1)
    back_local()
    w_loads[4].wait()
    w_loads[5].wait()

    arrived("S1")
    send("S2", xb.at[8 + away], xb.at[second], at_z(-ez))
    arrived("L2")
    send("L3", xb.at[middle * (OTHER + 5) + end * (10 + away)], xb.at[OTHER + 4], at_z(-ez))
    arrived("Y1")
    send("Y2", xb.at[pl.ds(4, 2)], xb.at[pl.ds(6, 2)], at_y(-ey))
    share_same(2)
    arrived("X1")
    send("X2", xb.at[pl.ds(12, 2)], xb.at[pl.ds(14, 2)], at_x(-ex))
    share_same(6)
    forward(2)
    forward(6)

    arrived("L3")
    send("L4", xb.at[OTHER + 4], xb.at[OTHER + 0], z_first)
    share_other(4)
    send("A1", xb.at[side], xb.at[8 + side], z_first)
    send("A2", xb.at[side], xb.at[10 + side], z_second)
    arrived("S2")
    share_other(5)
    arrived("Y2")
    share_same(3)
    arrived("X2")
    share_same(7)
    forward(3)
    forward(7)

    arrived("G")
    send("CH", gb.at[:, 2], gb.at[:, 3], sibling)
    for r in range(2):
        sb[TERM[5], r] = term(5, r, 2 * end).astype(BF16)
        send(f"R{r}", sb.at[TERM[5], r], rb.at[TERM[5], r], at_z(-ez))

    arrived("L4")
    send("OY1", xb.at[OTHER + 0], xb.at[OTHER + 2], at_y(ey))
    send("OX1", xb.at[OTHER + 0], xb.at[OTHER + 6], at_x(ex))
    share_other(0)
    for s in (3, 7, 2, 6):
        arrived(f"B{s}")
        add_terms(TERM[s])

    arrived("OY1")
    send("OY2", xb.at[OTHER + 2], xb.at[OTHER + 3], at_y(-ey))
    share_other(2)
    arrived("OX1")
    send("OX2", xb.at[OTHER + 6], xb.at[OTHER + 7], at_x(-ex))
    share_other(6)
    for r in range(2):
        arrived(f"R{r}")
        total = term(4, r).astype(BF16).astype(F32) + rb[TERM[5], r].astype(F32)
        sb[TERM[4], r] = total.astype(BF16)
        send(f"Q{r}", sb.at[TERM[4], r], rb.at[TERM[4], r], z_first)

    for name in ("C0", "CG", "CH", "D0"):
        arrived(name)
    weight_grad(0)
    weight_grad(1)
    for s in (2, 6):
        arrived(f"C{s}")
        arrived(f"D{s}")
        weight_grad(s)
    arrived("OY2")
    share_other(3)
    arrived("OX2")
    share_other(7)
    for s in (3, 7):
        arrived(f"C{s}")
        arrived(f"D{s}")
        weight_grad(s)

    arrived("A1")
    share_same(4)
    forward(4)
    arrived("A2")
    share_same(5)
    forward(5)
    for r in range(2):
        ob[0, r] = acc_o[r].astype(BF16)
        store = pltpu.make_async_copy(ob.at[0, r], out_ref.at[:, pl.ds(r * 512, 512)], o_sem.at[r])
        store.start()
        stores.append(store)
    for s in (4, 5):
        arrived(f"C{s}")
        arrived(f"D{s}")
        weight_grad(s)
    for r in range(2):
        arrived(f"Q{r}")
        ob[1, r] = (acc_g[r] + rb[TERM[4], r].astype(F32)).astype(BF16)
        store = pltpu.make_async_copy(ob.at[1, r], ig_ref.at[:, pl.ds(r * 512, 512)], o_sem.at[2 + r])
        store.start()
        stores.append(store)

    for name in NAMES:
        copies[name].wait_send()
    for store in stores:
        store.wait()


def body(inputs, weights, cotangent):
    n = len(NAMES)
    return pl.pallas_call(
        kernel,
        out_shape=(
            jax.ShapeDtypeStruct((256, 1024), BF16),
            jax.ShapeDtypeStruct((256, 1024), BF16),
            jax.ShapeDtypeStruct((2, 8, 128, 512), BF16),
        ),
        in_specs=[pl.BlockSpec(memory_space=pl.ANY)] * 3,
        out_specs=[pl.BlockSpec(memory_space=pl.ANY)] * 3,
        scratch_shapes=[
            pltpu.VMEM((24, 2, 2, 256, 128), BF16),
            pltpu.VMEM((8, 2, 2, 256, 128), BF16),
            pltpu.VMEM((8, 2, 512, 512), BF16),
            pltpu.VMEM((2, 4, 256, 512), BF16),
            pltpu.VMEM((6, 2, 256, 512), BF16),
            pltpu.VMEM((6, 2, 256, 512), BF16),
            pltpu.VMEM((2, 256, 512), F32),
            pltpu.VMEM((2, 256, 512), F32),
            pltpu.VMEM((2, 2, 256, 512), BF16),
            pltpu.VMEM((8, 2, 128, 512), BF16),
            pltpu.SemaphoreType.DMA((n,)),
            pltpu.SemaphoreType.DMA((n,)),
            pltpu.SemaphoreType.DMA((8,)),
            pltpu.SemaphoreType.DMA((2,)),
            pltpu.SemaphoreType.DMA((8,)),
            pltpu.SemaphoreType.DMA((12,)),
        ],
        compiler_params=pltpu.CompilerParams(
            collective_id=0, has_side_effects=True, vmem_limit_bytes=56 * 2**20
        ),
        cost_estimate=pl.CostEstimate(flops=6442450944, bytes_accessed=12 * 2**20, transcendentals=0),
    )(inputs, weights, cotangent)


def solution(mesh):
    in_specs = (P("dp", "feat"), P("feat", None, None, None), P("dp", "feat"))
    out_specs = (P("dp", "feat"), P("dp", "feat"), P("feat", None, "dp", None))
    return jax.shard_map(body, mesh=mesh, in_specs=in_specs, out_specs=out_specs, check_vma=False)
```

time: 236 us -> 95.4 us (0.40)
  waiting for transfers between devices: 138 us -> 0 us
  Pallas kernels: 0 us -> 89.4 us
  local copies, waits for them, and re-layouts: 34.9 us -> 5.21 us
  starting transfers between devices: 28.4 us -> 0 us
  matrix products: 19.3 us -> 0 us
  between operations: 14.1 us -> 0.65 us
    ppermute x12 -> x0, waiting for transfers between devices: 138 us -> none  [partner(): return lax.ppermute(value, axis, pairs)]
    pallas_call x0 -> x1, Pallas kernels: none -> 89.4 us  [body(): pl.pallas_call(kernel, out_shape=(jax.ShapeDtypeStruct((256, 1024), BF16)...]
    ppermute x12 -> x0, starting transfers between devices: 19.8 us -> none  [partner(): return lax.ppermute(value, axis, pairs)]
    dot_general x3 -> x0, matrix products: 19.3 us -> none  [the longest x1 6.98 us: body(): jnp.einsum('rsta,rsab->rtb', forward_stack, weights, preferred_element_ty...]
    all_to_all x2 -> x0, local copies, waits for them, and re-layouts: 15.1 us -> none  [body(): lax.all_to_all(forward_stack, 'dp', split_axis=3, concat_axis=2, tiled=True)]
    another operation x2 -> x0, local copies, waits for them, and re-layouts: 8.75 us -> none  [body(): jnp.stack([features] + [partner_rows[level] for level in range(levels)],...]
    all_to_all x1 -> x0, starting transfers between devices: 8.61 us -> none  [body(): lax.all_to_all(forward_stack, 'dp', split_axis=3, concat_axis=2, tiled=True)]
    unnamed x14 -> x5, local copies, waits for them, and re-layouts: 9.61 us -> 5.21 us
  transfers between devices with their start and end apart: 14 -> 0, of which waited for: 8 -> 0; matrix products, arithmetic and copies ran while one was open for 13% -> 0% of each run, Pallas kernels for 0% -> 0%
where the time goes in v1:
time: 95.4 us; the launch traced here: 95.3 us
  Pallas kernels  89.4 us (94%)
  local copies, waits for them, and re-layouts  5.21 us (5%)
    pallas_call x1, Pallas kernels, body(): pl.pallas_call(kernel, out_shape=(jax.ShapeDtypeStruct((256, 1024), BF16)...  89.4 us
    unnamed x5, local copies, waits for them, and re-layouts  5.21 us

profile of v1, /device:TPU:1, one launch (start us, length us, event | category | flops | bytes accessed | tf_op | source)
XLA Modules:
  0.0 95.3 jit_solution(11444354415548539496)
XLA Ops:
  0.6 89.4 %shard_map.58 = (bf16[256,1024]{1,0:T(8,128)(2,1)}, bf16[256,1024]{1,0:T(8,128)(2,1)}, bf16[2,8,128,512]{3,2,1,0:T(8,128)(2,1)}) custom-call(bf16[256,1024]{1,0:T(8,128)(2,1)} %x_ref.1, bf16[2,8,512,512]{3,2,1,0:T(8,128)(2,1)} %w_ref.1, bf16[256,1024]{1,0:T(8,128)(2,1)} %g_ref.1), custom_call_target="tpu_custom_call" | custom-call | flops 6442450944 | bytes 12582912 | tf_op jit(solution)/shard_map/pallas_call | solution.py:281
  90.1 0.0 copy-start
  90.1 2.0 %copy.9 = bf16[256,1024]{1,0:T(8,128)(2,1)} copy(bf16[256,1024]{1,0:T(8,128)(2,1)} %get-tuple-element.6) | data formatting | bytes 1048576
  92.1 1.9 %copy.10 = bf16[256,1024]{1,0:T(8,128)(2,1)} copy(bf16[256,1024]{1,0:T(8,128)(2,1)} %get-tuple-element.7) | data formatting | bytes 1048576
  93.9 0.0 copy-done
  94.0 1.3 %copy.11 = bf16[2,8,128,512]{3,2,1,0:T(8,128)(2,1)} copy(bf16[2,8,128,512]{3,2,1,0:T(8,128)(2,1)S(1)} %copy-done) | data formatting | bytes 4194304
Async XLA Ops:
  90.1 3.9 %copy-start = (bf16[2,8,128,512]{3,2,1,0:T(8,128)(2,1)S(1)}, bf16[2,8,128,512]{3,2,1,0:T(8,128)(2,1)}, u32[]{:S(2)}) copy-start(bf16[2,8,128,512]{3,2,1,0:T(8,128)(2,1)} %get-tuple-element.8) | copy-start | bytes 6291460

commit v2 on v1

--- a/solution.py
+++ b/solution.py
@@ -10,17 +10,18 @@
 F32 = jnp.float32
 OTHER = 16
 NAMES = (
-    ["S1", "S2", "L2", "L3", "L4", "G", "A1", "A2"]
+    ["GP1", "GM1", "GP2", "GM2", "GP3", "GM3", "GP4", "GM4", "S1", "S2", "L1", "L2", "L3", "L4", "A1P"]
     + ["Y1", "Y2", "X1", "X2", "OY1", "OY2", "OX1", "OX2"]
     + ["B2", "B3", "B6", "B7", "R0", "R1", "Q0", "Q1", "CG", "CH"]
     + [f"C{s}" for s in (0, 2, 3, 4, 5, 6, 7)]
     + [f"D{s}" for s in (0, 2, 3, 4, 5, 6, 7)]
 )
-IDS = {name: number for number, name in enumerate(NAMES)}
+MIDDLE = ["A1M", "A2P", "A2M"]
+IDS = {name: number for number, name in enumerate(NAMES + MIDDLE)}
 TERM = {2: 0, 3: 1, 6: 2, 7: 3, 5: 4, 4: 5}
 
 
-def kernel(x_ref, w_ref, g_ref, out_ref, ig_ref, dw_ref, xb, sx, wb, gb, rb, sb, acc_o, acc_g, ob, db,
+def kernel(x_ref, w_ref, g_ref, out_ref, ig_ref, dw_ref, xb, sx, wb, gb, gt, at, rb, sb, acc_o, acc_g, ob, db,
            send_sem, recv_sem, x_sem, g_sem, w_sem, o_sem):
     feat = lax.axis_index("feat")
     dp = lax.axis_index("dp")
@@ -49,8 +50,11 @@
 
     sibling = (feat, side * 2 + 1 - core)
     z_first = at_z(ez)
-    z_second = (x * 16 + ((z_lo + 2) % 4) * 4 + y, dp)
+    z_last = at_z(-ez)
+    odd = z % 2
+    even = 1 - odd
     second = end * (OTHER + 5) + middle * (10 + away)
+    mine = middle * (OTHER + 5) + end * (10 + away)
 
     loads = []
     for d in range(4):
@@ -71,22 +75,26 @@
         w_loads[s].start()
 
     barrier = pltpu.get_barrier_semaphore()
-    friends = [sibling, at_z(1), at_z(-1), at_z(2), at_z(-2), at_z(4), at_y(1), at_y(-1), at_y(2), at_x(1), at_x(-1), at_x(2)]
+    friends = [sibling, at_z(1), at_z(-1), at_y(1), at_y(-1), at_y(2), at_x(1), at_x(-1), at_x(2)]
     for friend in friends:
         pl.semaphore_signal(barrier, inc=1, device_id=friend, device_id_type=MESH)
     pl.semaphore_wait(barrier, len(friends))
 
-    copies = {}
-
-    def send(name, src, dst, device):
-        copies[name] = pltpu.make_async_remote_copy(
+    routes = {}
+
+    def descriptor(name):
+        src, dst, device = routes[name]
+        return pltpu.make_async_remote_copy(
             src_ref=src, dst_ref=dst, send_sem=send_sem.at[IDS[name]], recv_sem=recv_sem.at[IDS[name]],
             device_id=device, device_id_type=MESH,
         )
-        copies[name].start()
+
+    def send(name, src, dst, device):
+        routes[name] = (src, dst, device)
+        descriptor(name).start()
 
     def arrived(name):
-        copies[name].wait_recv()
+        descriptor(name).wait_recv()
 
     def share_same(s):
         send(f"C{s}", xb.at[2 * s + side, 1 - core], sx.at[s, 0], sibling)
@@ -132,6 +140,20 @@
             return carry
 
         lax.fori_loop(0, 2, row, 0)
+
+    for r in range(2):
+        routes[f"R{r}"] = (sb.at[TERM[5], r], rb.at[TERM[5], r], z_last)
+        routes[f"Q{r}"] = (sb.at[TERM[4], r], rb.at[TERM[4], r], z_first)
+
+    def relay(r, q):
+        sb[TERM[5], r] = term(5, r, q).astype(BF16)
+        descriptor(f"R{r}").start()
+
+    def add_and_pass(r):
+        arrived(f"R{r}")
+        total = term(4, r).astype(BF16).astype(F32) + rb[TERM[5], r].astype(F32)
+        sb[TERM[4], r] = total.astype(BF16)
+        descriptor(f"Q{r}").start()
 
     stores = []
 
@@ -154,15 +176,20 @@
         store.start()
         stores.append(store)
 
+    routes["A1M"] = (xb.at[side], at.at[1], z_last)
+    routes["A2P"] = (at.at[1], xb.at[10 + side], z_first)
+    routes["A2M"] = (xb.at[8 + side], xb.at[10 + side], z_last)
+
+    for load in g_loads:
+        load.wait()
+    send("GP1", gb.at[odd, 0], gt.at[0, 0], z_first)
+    send("GM1", gb.at[even, 0], gt.at[1, 0], z_last)
     for load in loads:
         load.wait()
     send("S1", xb.at[away], xb.at[8 + away], z_first)
-    send("L2", xb.at[away], xb.at[second], at_z(-2 * ez))
+    send("L1", xb.at[away], at.at[0], z_last)
     send("Y1", xb.at[pl.ds(0, 2)], xb.at[pl.ds(4, 2)], at_y(ey))
     send("X1", xb.at[pl.ds(0, 2)], xb.at[pl.ds(12, 2)], at_x(ex))
-    for load in g_loads:
-        load.wait()
-    send("G", gb.at[:, 0], gb.at[:, 2], at_z(4))
     share_same(0)
     send("CG", gb.at[:, 0], gb.at[:, 1], sibling)
 
@@ -170,72 +197,103 @@
         w_loads[s].wait()
         back(s)
         send(f"B{s}", sb.at[TERM[s]], rb.at[TERM[s]], device)
-    w_loads[0].wait()
-    w_loads[1].wait()
+    for s in (5, 4, 0, 1):
+        w_loads[s].wait()
+
+    arrived("GP1")
+    send("GM2", gt.at[0, 0], gt.at[1, 1], z_last)
+    arrived("GM1")
+    send("GP2", gt.at[1, 0], gt.at[0, 1], z_first)
     forward(0, start=True)
     forward(1)
+    arrived("S1")
+    send("S2", xb.at[8 + away], xb.at[second], z_last)
+    arrived("L1")
+    send("L2", at.at[0], xb.at[second], z_first)
     back_local()
-    w_loads[4].wait()
-    w_loads[5].wait()
-
-    arrived("S1")
-    send("S2", xb.at[8 + away], xb.at[second], at_z(-ez))
-    arrived("L2")
-    send("L3", xb.at[middle * (OTHER + 5) + end * (10 + away)], xb.at[OTHER + 4], at_z(-ez))
     arrived("Y1")
     send("Y2", xb.at[pl.ds(4, 2)], xb.at[pl.ds(6, 2)], at_y(-ey))
     share_same(2)
     arrived("X1")
     send("X2", xb.at[pl.ds(12, 2)], xb.at[pl.ds(14, 2)], at_x(-ex))
     share_same(6)
+
+    arrived("GP2")
+    send("GM3", gt.at[0, 1], gt.at[1, 2], z_last)
+    arrived("GM2")
+    send("GP3", gt.at[1, 1], gt.at[0, 2], z_first)
+    send("A1P", xb.at[side], xb.at[8 + side], z_first)
     forward(2)
     forward(6)
-
-    arrived("L3")
-    send("L4", xb.at[OTHER + 4], xb.at[OTHER + 0], z_first)
-    share_other(4)
-    send("A1", xb.at[side], xb.at[8 + side], z_first)
-    send("A2", xb.at[side], xb.at[10 + side], z_second)
+    arrived("L2")
+    send("L3", xb.at[mine], xb.at[OTHER + 4], z_last)
     arrived("S2")
     share_other(5)
     arrived("Y2")
     share_same(3)
     arrived("X2")
     share_same(7)
+
+    arrived("GP3")
+    send("GM4", gt.at[0, 2], gb.at[even, 2], z_last)
+    arrived("GM3")
+    send("GP4", gt.at[1, 2], gb.at[odd, 2], z_first)
     forward(3)
     forward(7)
-
-    arrived("G")
+    arrived("L3")
+    send("L4", xb.at[OTHER + 4], xb.at[OTHER + 0], z_first)
+    share_other(4)
+
+    @pl.when(middle == 1)
+    def _():
+        descriptor("A1M").start()
+        relay(0, 0)
+        relay(1, 0)
+
+    arrived("A1P")
+
+    @pl.when(middle == 1)
+    def _():
+        descriptor("A2M").start()
+
+    share_same(4)
+    arrived("GP4")
+    arrived("GM4")
+
+    @pl.when(end == 1)
+    def _():
+        relay(0, 2)
+        relay(1, 2)
+
     send("CH", gb.at[:, 2], gb.at[:, 3], sibling)
-    for r in range(2):
-        sb[TERM[5], r] = term(5, r, 2 * end).astype(BF16)
-        send(f"R{r}", sb.at[TERM[5], r], rb.at[TERM[5], r], at_z(-ez))
+    forward(4)
+    for s in (3, 7, 2, 6):
+        arrived(f"B{s}")
+        add_terms(TERM[s])
 
     arrived("L4")
     send("OY1", xb.at[OTHER + 0], xb.at[OTHER + 2], at_y(ey))
     send("OX1", xb.at[OTHER + 0], xb.at[OTHER + 6], at_x(ex))
     share_other(0)
-    for s in (3, 7, 2, 6):
-        arrived(f"B{s}")
-        add_terms(TERM[s])
-
+
+    @pl.when(middle == 1)
+    def _():
+        arrived("A1M")
+        descriptor("A2P").start()
+
+    add_and_pass(0)
+    for name in ("C0", "CG", "CH", "D0"):
+        arrived(name)
+    weight_grad(0)
     arrived("OY1")
     send("OY2", xb.at[OTHER + 2], xb.at[OTHER + 3], at_y(-ey))
     share_other(2)
     arrived("OX1")
     send("OX2", xb.at[OTHER + 6], xb.at[OTHER + 7], at_x(-ex))
     share_other(6)
-    for r in range(2):
-        arrived(f"R{r}")
-        total = term(4, r).astype(BF16).astype(F32) + rb[TERM[5], r].astype(F32)
-        sb[TERM[4], r] = total.astype(BF16)
-        send(f"Q{r}", sb.at[TERM[4], r], rb.at[TERM[4], r], z_first)
-
-    for name in ("C0", "CG", "CH", "D0"):
-        arrived(name)
-    weight_grad(0)
+    add_and_pass(1)
     weight_grad(1)
-    for s in (2, 6):
+    for s in (4, 2, 6):
         arrived(f"C{s}")
         arrived(f"D{s}")
         weight_grad(s)
@@ -243,15 +301,15 @@
     share_other(3)
     arrived("OX2")
     share_other(7)
-    for s in (3, 7):
-        arrived(f"C{s}")
-        arrived(f"D{s}")
-        weight_grad(s)
-
-    arrived("A1")
-    share_same(4)
-    forward(4)
-    arrived("A2")
+
+    @pl.when(end == 1)
+    def _():
+        arrived("A2P")
+
+    @pl.when(middle == 1)
+    def _():
+        arrived("A2M")
+
     share_same(5)
     forward(5)
     for r in range(2):
@@ -259,7 +317,7 @@
         store = pltpu.make_async_copy(ob.at[0, r], out_ref.at[:, pl.ds(r * 512, 512)], o_sem.at[r])
         store.start()
         stores.append(store)
-    for s in (4, 5):
+    for s in (3, 7, 5):
         arrived(f"C{s}")
         arrived(f"D{s}")
         weight_grad(s)
@@ -271,13 +329,19 @@
         stores.append(store)
 
     for name in NAMES:
-        copies[name].wait_send()
+        descriptor(name).wait_send()
+
+    @pl.when(middle == 1)
+    def _():
+        for name in MIDDLE:
+            descriptor(name).wait_send()
+
     for store in stores:
         store.wait()
 
 
 def body(inputs, weights, cotangent):
-    n = len(NAMES)
+    n = len(NAMES + MIDDLE)
     return pl.pallas_call(
         kernel,
         out_shape=(
@@ -292,6 +356,8 @@
             pltpu.VMEM((8, 2, 2, 256, 128), BF16),
             pltpu.VMEM((8, 2, 512, 512), BF16),
             pltpu.VMEM((2, 4, 256, 512), BF16),
+            pltpu.VMEM((2, 3, 256, 512), BF16),
+            pltpu.VMEM((2, 2, 2, 256, 128), BF16),
             pltpu.VMEM((6, 2, 256, 512), BF16),
             pltpu.VMEM((6, 2, 256, 512), BF16),
             pltpu.VMEM((2, 256, 512), F32),

time: 95.4 us -> 83.3 us (0.87)
  Pallas kernels: 89.4 us -> 77.3 us
    pallas_call x1, Pallas kernels: 89.4 us -> 77.3 us  [body(): pl.pallas_call(kernel, out_shape=(jax.ShapeDtypeStruct((256, 1024), BF16)...]
where the time goes in v2:
time: 83.3 us; the launch traced here: 83.2 us
  Pallas kernels  77.3 us (93%)
  local copies, waits for them, and re-layouts  5.21 us (6%)
    pallas_call x1, Pallas kernels, body(): pl.pallas_call(kernel, out_shape=(jax.ShapeDtypeStruct((256, 1024), BF16)...  77.3 us
    unnamed x5, local copies, waits for them, and re-layouts  5.21 us

profile of v2, /device:TPU:1, one launch (start us, length us, event | category | flops | bytes accessed | tf_op | source)
XLA Modules:
  0.0 83.2 jit_solution(5989251106380620018)
XLA Ops:
  0.6 77.3 %shard_map.58 = (bf16[256,1024]{1,0:T(8,128)(2,1)}, bf16[256,1024]{1,0:T(8,128)(2,1)}, bf16[2,8,128,512]{3,2,1,0:T(8,128)(2,1)}) custom-call(bf16[256,1024]{1,0:T(8,128)(2,1)} %x_ref.1, bf16[2,8,512,512]{3,2,1,0:T(8,128)(2,1)} %w_ref.1, bf16[256,1024]{1,0:T(8,128)(2,1)} %g_ref.1), custom_call_target="tpu_custom_call" | custom-call | flops 6442450944 | bytes 12582912 | tf_op jit(solution)/shard_map/pallas_call | solution.py:345
  78.0 0.0 copy-start
  78.0 2.0 %copy.9 = bf16[256,1024]{1,0:T(8,128)(2,1)} copy(bf16[256,1024]{1,0:T(8,128)(2,1)} %get-tuple-element.6) | data formatting | bytes 1048576
  80.0 1.9 %copy.10 = bf16[256,1024]{1,0:T(8,128)(2,1)} copy(bf16[256,1024]{1,0:T(8,128)(2,1)} %get-tuple-element.7) | data formatting | bytes 1048576
  81.8 0.0 copy-done
  81.9 1.3 %copy.11 = bf16[2,8,128,512]{3,2,1,0:T(8,128)(2,1)} copy(bf16[2,8,128,512]{3,2,1,0:T(8,128)(2,1)S(1)} %copy-done) | data formatting | bytes 4194304
Async XLA Ops:
  78.0 3.9 %copy-start = (bf16[2,8,128,512]{3,2,1,0:T(8,128)(2,1)S(1)}, bf16[2,8,128,512]{3,2,1,0:T(8,128)(2,1)}, u32[]{:S(2)}) copy-start(bf16[2,8,128,512]{3,2,1,0:T(8,128)(2,1)} %get-tuple-element.8) | copy-start | bytes 6291460

commit v3 on v2

--- a/solution.py
+++ b/solution.py
@@ -21,8 +21,8 @@
 TERM = {2: 0, 3: 1, 6: 2, 7: 3, 5: 4, 4: 5}
 
 
-def kernel(x_ref, w_ref, g_ref, out_ref, ig_ref, dw_ref, xb, sx, wb, gb, gt, at, rb, sb, acc_o, acc_g, ob, db,
-           send_sem, recv_sem, x_sem, g_sem, w_sem, o_sem):
+def kernel(x_ref, w_ref, g_ref, out_ref, ig_ref, dw_ref, xb, sx, wb, gb, gt, at, rb, sb, acc_o, acc_g,
+           send_sem, recv_sem, x_sem, g_sem, w_sem):
     feat = lax.axis_index("feat")
     dp = lax.axis_index("dp")
     y = feat % 4
@@ -155,8 +155,6 @@
         sb[TERM[4], r] = total.astype(BF16)
         descriptor(f"Q{r}").start()
 
-    stores = []
-
     def weight_grad(s):
         base = 0 if s == 1 else s
 
@@ -168,13 +166,10 @@
             total = lax.dot_general(
                 tokens, gb[r].reshape(1024, 512), (((0,), (0,)), ((), ())), preferred_element_type=F32
             )
-            db[s, r] = total.astype(BF16)
-            return carry
-
-        lax.fori_loop(0, 2, row, 0)
-        store = pltpu.make_async_copy(db.at[s], dw_ref.at[:, s], o_sem.at[4 + s])
-        store.start()
-        stores.append(store)
+            dw_ref[r, s] = total.astype(BF16)
+            return carry
+
+        lax.fori_loop(0, 2, row, 0)
 
     routes["A1M"] = (xb.at[side], at.at[1], z_last)
     routes["A2P"] = (at.at[1], xb.at[10 + side], z_first)
@@ -313,20 +308,14 @@
     share_same(5)
     forward(5)
     for r in range(2):
-        ob[0, r] = acc_o[r].astype(BF16)
-        store = pltpu.make_async_copy(ob.at[0, r], out_ref.at[:, pl.ds(r * 512, 512)], o_sem.at[r])
-        store.start()
-        stores.append(store)
+        out_ref[:, pl.ds(r * 512, 512)] = acc_o[r].astype(BF16)
     for s in (3, 7, 5):
         arrived(f"C{s}")
         arrived(f"D{s}")
         weight_grad(s)
     for r in range(2):
         arrived(f"Q{r}")
-        ob[1, r] = (acc_g[r] + rb[TERM[4], r].astype(F32)).astype(BF16)
-        store = pltpu.make_async_copy(ob.at[1, r], ig_ref.at[:, pl.ds(r * 512, 512)], o_sem.at[2 + r])
-        store.start()
-        stores.append(store)
+        ig_ref[:, pl.ds(r * 512, 512)] = (acc_g[r] + rb[TERM[4], r].astype(F32)).astype(BF16)
 
     for name in NAMES:
         descriptor(name).wait_send()
@@ -336,21 +325,34 @@
         for name in MIDDLE:
             descriptor(name).wait_send()
 
-    for store in stores:
-        store.wait()
+
+def settle(out_in, ig_in, dw_in, out_ref, ig_ref, dw_ref, sem):
+    moves = []
+    for r in range(2):
+        for s in range(0, 8, 4):
+            slots = pl.ds(s, 4)
+            moves.append((dw_in.at[r, slots], dw_ref.at[r, slots]))
+        rows = pl.ds(r * 128, 128)
+        moves.append((out_in.at[rows], out_ref.at[rows]))
+        moves.append((ig_in.at[rows], ig_ref.at[rows]))
+    moves = [pltpu.make_async_copy(src, dst, sem.at[k]) for k, (src, dst) in enumerate(moves)]
+    for move in moves:
+        move.start()
+    for move in moves:
+        move.wait()
 
 
 def body(inputs, weights, cotangent):
     n = len(NAMES + MIDDLE)
-    return pl.pallas_call(
+    results = pl.pallas_call(
         kernel,
         out_shape=(
-            jax.ShapeDtypeStruct((256, 1024), BF16),
-            jax.ShapeDtypeStruct((256, 1024), BF16),
-            jax.ShapeDtypeStruct((2, 8, 128, 512), BF16),
+            pltpu.VMEM((256, 1024), BF16),
+            pltpu.VMEM((256, 1024), BF16),
+            pltpu.VMEM((2, 8, 128, 512), BF16),
         ),
         in_specs=[pl.BlockSpec(memory_space=pl.ANY)] * 3,
-        out_specs=[pl.BlockSpec(memory_space=pl.ANY)] * 3,
+        out_specs=[pl.BlockSpec(memory_space=pltpu.VMEM)] * 3,
         scratch_shapes=[
             pltpu.VMEM((24, 2, 2, 256, 128), BF16),
             pltpu.VMEM((8, 2, 2, 256, 128), BF16),
@@ -362,20 +364,25 @@
             pltpu.VMEM((6, 2, 256, 512), BF16),
             pltpu.VMEM((2, 256, 512), F32),
             pltpu.VMEM((2, 256, 512), F32),
-            pltpu.VMEM((2, 2, 256, 512), BF16),
-            pltpu.VMEM((8, 2, 128, 512), BF16),
             pltpu.SemaphoreType.DMA((n,)),
             pltpu.SemaphoreType.DMA((n,)),
             pltpu.SemaphoreType.DMA((8,)),
             pltpu.SemaphoreType.DMA((2,)),
             pltpu.SemaphoreType.DMA((8,)),
-            pltpu.SemaphoreType.DMA((12,)),
         ],
         compiler_params=pltpu.CompilerParams(
             collective_id=0, has_side_effects=True, vmem_limit_bytes=56 * 2**20
         ),
         cost_estimate=pl.CostEstimate(flops=6442450944, bytes_accessed=12 * 2**20, transcendentals=0),
     )(inputs, weights, cotangent)
+    return pl.pallas_call(
+        settle,
+        out_shape=tuple(jax.ShapeDtypeStruct(result.shape, result.dtype) for result in results),
+        in_specs=[pl.BlockSpec(memory_space=pl.ANY)] * 3,
+        out_specs=[pl.BlockSpec(memory_space=pl.ANY)] * 3,
+        scratch_shapes=[pltpu.SemaphoreType.DMA((8,))],
+        compiler_params=pltpu.CompilerParams(vmem_limit_bytes=8 * 2**20),
+    )(*results)
 
 
 def solution(mesh):

time: 83.3 us -> 78.9 us (0.947)
  local copies, waits for them, and re-layouts: 5.21 us -> 0 us
  Pallas kernels: 77.3 us -> 78.2 us
    unnamed x5 -> x0, local copies, waits for them, and re-layouts: 5.21 us -> none
    pallas_call x1 -> x2, Pallas kernels: 77.3 us -> 78.2 us  [the longest x1 76.5 us: body(): pl.pallas_call(kernel, out_shape=(pltpu.VMEM((256, 1024), BF16), pltpu.VM...]
where the time goes in v3:
time: 78.9 us; the launch traced here: 78.8 us
  Pallas kernels  78.2 us (99%)
    pallas_call x1, Pallas kernels, body(): pl.pallas_call(kernel, out_shape=(pltpu.VMEM((256, 1024), BF16), pltpu.VM...  76.5 us
    pallas_call x1, Pallas kernels, body(): pl.pallas_call(settle, out_shape=tuple((jax.ShapeDtypeStruct(result.shape...  1.72 us

profile of v3, /device:TPU:1, one launch (start us, length us, event | category | flops | bytes accessed | tf_op | source)
XLA Modules:
  0.0 78.8 jit_solution(1587809356326222606)
XLA Ops:
  0.6 76.5 %shard_map.58 = (bf16[256,1024]{1,0:T(8,128)(2,1)S(1)}, bf16[256,1024]{1,0:T(8,128)(2,1)S(1)}, bf16[2,8,128,512]{3,2,1,0:T(8,128)(2,1)S(1)}) custom-call(bf16[256,1024]{1,0:T(8,128)(2,1)} %x_ref.1, bf16[2,8,512,512]{3,2,1,0:T(8,128)(2,1)} %w_ref.1, bf16[256,1024]{1,0:T(8,128)(2,1)} %g_ref.1), custom_call_target="tpu_custom_call" | custom-call | flops 6442450944 | bytes 12582912 | tf_op jit(solution)/shard_map/pallas_call | solution.py:347
  77.1 1.7 %shard_map.59 = (bf16[256,1024]{1,0:T(8,128)(2,1)}, bf16[256,1024]{1,0:T(8,128)(2,1)}, bf16[2,8,128,512]{3,2,1,0:T(8,128)(2,1)}) custom-call(bf16[256,1024]{1,0:T(8,128)(2,1)S(1)} %get-tuple-element.6.out_in, bf16[256,1024]{1,0:T(8,128)(2,1)S(1)} %get-tuple-element.7.ig_in, bf16[2,8,128,512]{3,2,1,0:T(8,128)(2,1)S(1)} %get-tuple-element.8.dw_in), custom_call_target="tpu_custom_call" | custom-call | tf_op jit(solution)/shard_map/pallas_call | solution.py:378

commit v4 on v3

--- a/solution.py
+++ b/solution.py
@@ -12,7 +12,7 @@
 NAMES = (
     ["GP1", "GM1", "GP2", "GM2", "GP3", "GM3", "GP4", "GM4", "S1", "S2", "L1", "L2", "L3", "L4", "A1P"]
     + ["Y1", "Y2", "X1", "X2", "OY1", "OY2", "OX1", "OX2"]
-    + ["B2", "B3", "B6", "B7", "R0", "R1", "Q0", "Q1", "CG", "CH"]
+    + ["B2", "B3", "B6", "B7", "R0", "R1", "R2", "R3", "Q0", "Q1", "Q2", "Q3", "CG", "CH"]
     + [f"C{s}" for s in (0, 2, 3, 4, 5, 6, 7)]
     + [f"D{s}" for s in (0, 2, 3, 4, 5, 6, 7)]
 )
@@ -56,6 +56,15 @@
     second = end * (OTHER + 5) + middle * (10 + away)
     mine = middle * (OTHER + 5) + end * (10 + away)
 
+    barrier = pltpu.get_barrier_semaphore()
+    friends = [sibling, at_z(1), at_z(-1), at_y(1), at_y(-1), at_y(2), at_x(1), at_x(-1), at_x(2)]
+    for friend in friends:
+        pl.semaphore_signal(barrier, inc=1, device_id=friend, device_id_type=MESH)
+    g_loads = []
+    for r in range(2):
+        load = pltpu.make_async_copy(g_ref.at[:, pl.ds(r * 512, 512)], gb.at[r, 0], g_sem.at[r])
+        load.start()
+        g_loads.append(load)
     loads = []
     for d in range(4):
         for r in range(2):
@@ -64,20 +73,6 @@
             )
             load.start()
             loads.append(load)
-    g_loads = []
-    for r in range(2):
-        load = pltpu.make_async_copy(g_ref.at[:, pl.ds(r * 512, 512)], gb.at[r, 0], g_sem.at[r])
-        load.start()
-        g_loads.append(load)
-    w_loads = {}
-    for s in (3, 7, 2, 6, 0, 1, 4, 5):
-        w_loads[s] = pltpu.make_async_copy(w_ref.at[:, s], wb.at[s], w_sem.at[s])
-        w_loads[s].start()
-
-    barrier = pltpu.get_barrier_semaphore()
-    friends = [sibling, at_z(1), at_z(-1), at_y(1), at_y(-1), at_y(2), at_x(1), at_x(-1), at_x(2)]
-    for friend in friends:
-        pl.semaphore_signal(barrier, inc=1, device_id=friend, device_id_type=MESH)
     pl.semaphore_wait(barrier, len(friends))
 
     routes = {}
@@ -142,18 +137,23 @@
         lax.fori_loop(0, 2, row, 0)
 
     for r in range(2):
-        routes[f"R{r}"] = (sb.at[TERM[5], r], rb.at[TERM[5], r], z_last)
-        routes[f"Q{r}"] = (sb.at[TERM[4], r], rb.at[TERM[4], r], z_first)
+        for h in range(2):
+            rows = pl.ds(h * 128, 128)
+            routes[f"R{2 * r + h}"] = (sb.at[TERM[5], r, rows], rb.at[TERM[5], r, rows], z_last)
+            routes[f"Q{2 * r + h}"] = (sb.at[TERM[4], r, rows], rb.at[TERM[4], r, rows], z_first)
 
     def relay(r, q):
         sb[TERM[5], r] = term(5, r, q).astype(BF16)
-        descriptor(f"R{r}").start()
+        for h in range(2):
+            descriptor(f"R{2 * r + h}").start()
 
     def add_and_pass(r):
-        arrived(f"R{r}")
-        total = term(4, r).astype(BF16).astype(F32) + rb[TERM[5], r].astype(F32)
-        sb[TERM[4], r] = total.astype(BF16)
-        descriptor(f"Q{r}").start()
+        for h in range(2):
+            rows = pl.ds(h * 128, 128)
+            arrived(f"R{2 * r + h}")
+            total = sb[TERM[4], r, rows].astype(F32) + rb[TERM[5], r, rows].astype(F32)
+            sb[TERM[4], r, rows] = total.astype(BF16)
+            descriptor(f"Q{2 * r + h}").start()
 
     def weight_grad(s):
         base = 0 if s == 1 else s
@@ -171,6 +171,7 @@
 
         lax.fori_loop(0, 2, row, 0)
 
+    routes["CH"] = (gb.at[:, 2], gb.at[:, 3], sibling)
     routes["A1M"] = (xb.at[side], at.at[1], z_last)
     routes["A2P"] = (at.at[1], xb.at[10 + side], z_first)
     routes["A2M"] = (xb.at[8 + side], xb.at[10 + side], z_last)
@@ -187,6 +188,10 @@
     send("X1", xb.at[pl.ds(0, 2)], xb.at[pl.ds(12, 2)], at_x(ex))
     share_same(0)
     send("CG", gb.at[:, 0], gb.at[:, 1], sibling)
+    w_loads = {}
+    for s in (3, 7, 2, 6, 0, 1, 4, 5):
+        w_loads[s] = pltpu.make_async_copy(w_ref.at[:, s], wb.at[s], w_sem.at[s])
+        w_loads[s].start()
 
     for s, device in ((3, at_y(2)), (7, at_x(2)), (2, at_y(ey)), (6, at_x(ex))):
         w_loads[s].wait()
@@ -206,6 +211,7 @@
     arrived("L1")
     send("L2", at.at[0], xb.at[second], z_first)
     back_local()
+    back(4)
     arrived("Y1")
     send("Y2", xb.at[pl.ds(4, 2)], xb.at[pl.ds(6, 2)], at_y(-ey))
     share_same(2)
@@ -222,6 +228,12 @@
     forward(6)
     arrived("L2")
     send("L3", xb.at[mine], xb.at[OTHER + 4], z_last)
+
+    @pl.when(middle == 1)
+    def _():
+        descriptor("A1M").start()
+        relay(0, 0)
+
     arrived("S2")
     share_other(5)
     arrived("Y2")
@@ -233,18 +245,16 @@
     send("GM4", gt.at[0, 2], gb.at[even, 2], z_last)
     arrived("GM3")
     send("GP4", gt.at[1, 2], gb.at[odd, 2], z_first)
+
+    @pl.when(middle == 1)
+    def _():
+        relay(1, 0)
+
     forward(3)
     forward(7)
     arrived("L3")
     send("L4", xb.at[OTHER + 4], xb.at[OTHER + 0], z_first)
     share_other(4)
-
-    @pl.when(middle == 1)
-    def _():
-        descriptor("A1M").start()
-        relay(0, 0)
-        relay(1, 0)
-
     arrived("A1P")
 
     @pl.when(middle == 1)
@@ -253,14 +263,19 @@
 
     share_same(4)
     arrived("GP4")
-    arrived("GM4")
+
+    @pl.when(middle == 1)
+    def _():
+        arrived("A1M")
+        descriptor("A2P").start()
 
     @pl.when(end == 1)
     def _():
+        arrived("GM4")
         relay(0, 2)
         relay(1, 2)
-
-    send("CH", gb.at[:, 2], gb.at[:, 3], sibling)
+        descriptor("CH").start()
+
     forward(4)
     for s in (3, 7, 2, 6):
         arrived(f"B{s}")
@@ -270,22 +285,22 @@
     send("OY1", xb.at[OTHER + 0], xb.at[OTHER + 2], at_y(ey))
     send("OX1", xb.at[OTHER + 0], xb.at[OTHER + 6], at_x(ex))
     share_other(0)
-
-    @pl.when(middle == 1)
-    def _():
-        arrived("A1M")
-        descriptor("A2P").start()
-
     add_and_pass(0)
-    for name in ("C0", "CG", "CH", "D0"):
-        arrived(name)
-    weight_grad(0)
+
+    @pl.when(middle == 1)
+    def _():
+        arrived("GM4")
+        descriptor("CH").start()
+
     arrived("OY1")
     send("OY2", xb.at[OTHER + 2], xb.at[OTHER + 3], at_y(-ey))
     share_other(2)
     arrived("OX1")
     send("OX2", xb.at[OTHER + 6], xb.at[OTHER + 7], at_x(-ex))
     share_other(6)
+    for name in ("C0", "CG", "CH", "D0"):
+        arrived(name)
+    weight_grad(0)
     add_and_pass(1)
     weight_grad(1)
     for s in (4, 2, 6):
@@ -314,7 +329,8 @@
         arrived(f"D{s}")
         weight_grad(s)
     for r in range(2):
-        arrived(f"Q{r}")
+        arrived(f"Q{2 * r}")
+        arrived(f"Q{2 * r + 1}")
         ig_ref[:, pl.ds(r * 512, 512)] = (acc_g[r] + rb[TERM[4], r].astype(F32)).astype(BF16)
 
     for name in NAMES:

time: 78.9 us -> 77.8 us (0.986); the launches traced: 78.8 us -> 76.6 us
  Pallas kernels: 78.2 us -> 76 us
    pallas_call x1, Pallas kernels: 76.5 us -> 74.3 us  [body(): pl.pallas_call(kernel, out_shape=(pltpu.VMEM((256, 1024), BF16), pltpu.VM...]
where the time goes in v4:
time: 77.8 us; the launch traced here: 76.6 us
  Pallas kernels  76 us (98%)
    pallas_call x1, Pallas kernels, body(): pl.pallas_call(kernel, out_shape=(pltpu.VMEM((256, 1024), BF16), pltpu.VM...  74.3 us
    pallas_call x1, Pallas kernels, body(): pl.pallas_call(settle, out_shape=tuple((jax.ShapeDtypeStruct(result.shape...  1.72 us

profile of v4, /device:TPU:1, one launch (start us, length us, event | category | flops | bytes accessed | tf_op | source)
XLA Modules:
  0.0 76.6 jit_solution(767729965449293760)
XLA Ops:
  0.6 74.3 %shard_map.58 = (bf16[256,1024]{1,0:T(8,128)(2,1)S(1)}, bf16[256,1024]{1,0:T(8,128)(2,1)S(1)}, bf16[2,8,128,512]{3,2,1,0:T(8,128)(2,1)S(1)}) custom-call(bf16[256,1024]{1,0:T(8,128)(2,1)} %x_ref.1, bf16[2,8,512,512]{3,2,1,0:T(8,128)(2,1)} %w_ref.1, bf16[256,1024]{1,0:T(8,128)(2,1)} %g_ref.1), custom_call_target="tpu_custom_call" | custom-call | flops 6442450944 | bytes 12582912 | tf_op jit(solution)/shard_map/pallas_call | solution.py:363
  74.9 1.7 %shard_map.59 = (bf16[256,1024]{1,0:T(8,128)(2,1)}, bf16[256,1024]{1,0:T(8,128)(2,1)}, bf16[2,8,128,512]{3,2,1,0:T(8,128)(2,1)}) custom-call(bf16[256,1024]{1,0:T(8,128)(2,1)S(1)} %get-tuple-element.6.out_in, bf16[256,1024]{1,0:T(8,128)(2,1)S(1)} %get-tuple-element.7.ig_in, bf16[2,8,128,512]{3,2,1,0:T(8,128)(2,1)S(1)} %get-tuple-element.8.dw_in), custom_call_target="tpu_custom_call" | custom-call | tf_op jit(solution)/shard_map/pallas_call | solution.py:394

commit v5 on v4

--- a/solution.py
+++ b/solution.py
@@ -10,8 +10,9 @@
 F32 = jnp.float32
 OTHER = 16
 NAMES = (
-    ["GP1", "GM1", "GP2", "GM2", "GP3", "GM3", "GP4", "GM4", "S1", "S2", "L1", "L2", "L3", "L4", "A1P"]
-    + ["Y1", "Y2", "X1", "X2", "OY1", "OY2", "OX1", "OX2"]
+    ["GP1", "GM1", "GP2", "GM2", "GP3", "GM3", "GP4", "GM4", "S1", "S2", "L1", "L2", "L3", "L4a", "L4b", "A1P"]
+    + ["Y1", "Y2", "X1", "X2"]
+    + [f"O{axis}{hop}{part}" for axis in "XY" for hop in (1, 2) for part in "ab"]
     + ["B2", "B3", "B6", "B7", "R0", "R1", "R2", "R3", "Q0", "Q1", "Q2", "Q3", "CG", "CH"]
     + [f"C{s}" for s in (0, 2, 3, 4, 5, 6, 7)]
     + [f"D{s}" for s in (0, 2, 3, 4, 5, 6, 7)]
@@ -91,6 +92,10 @@
     def arrived(name):
         descriptor(name).wait_recv()
 
+    def send_half(name, here, there, part, device):
+        column = 1 - core if part == "a" else core
+        send(name + part, xb.at[OTHER + here, column], xb.at[OTHER + there, column], device)
+
     def share_same(s):
         send(f"C{s}", xb.at[2 * s + side, 1 - core], sx.at[s, 0], sibling)
 
@@ -253,7 +258,8 @@
     forward(3)
     forward(7)
     arrived("L3")
-    send("L4", xb.at[OTHER + 4], xb.at[OTHER + 0], z_first)
+    send_half("L4", 4, 0, "a", z_first)
+    send_half("L4", 4, 0, "b", z_first)
     share_other(4)
     arrived("A1P")
 
@@ -281,10 +287,12 @@
         arrived(f"B{s}")
         add_terms(TERM[s])
 
-    arrived("L4")
-    send("OY1", xb.at[OTHER + 0], xb.at[OTHER + 2], at_y(ey))
-    send("OX1", xb.at[OTHER + 0], xb.at[OTHER + 6], at_x(ex))
-    share_other(0)
+    for part in "ab":
+        arrived(f"L4{part}")
+        send_half("OY1", 0, 2, part, at_y(ey))
+        send_half("OX1", 0, 6, part, at_x(ex))
+        if part == "a":
+            share_other(0)
     add_and_pass(0)
 
     @pl.when(middle == 1)
@@ -292,12 +300,14 @@
         arrived("GM4")
         descriptor("CH").start()
 
-    arrived("OY1")
-    send("OY2", xb.at[OTHER + 2], xb.at[OTHER + 3], at_y(-ey))
-    share_other(2)
-    arrived("OX1")
-    send("OX2", xb.at[OTHER + 6], xb.at[OTHER + 7], at_x(-ex))
-    share_other(6)
+    for part in "ab":
+        arrived(f"OY1{part}")
+        send_half("OY2", 2, 3, part, at_y(-ey))
+        arrived(f"OX1{part}")
+        send_half("OX2", 6, 7, part, at_x(-ex))
+        if part == "a":
+            share_other(2)
+            share_other(6)
     for name in ("C0", "CG", "CH", "D0"):
         arrived(name)
     weight_grad(0)
@@ -307,10 +317,12 @@
         arrived(f"C{s}")
         arrived(f"D{s}")
         weight_grad(s)
-    arrived("OY2")
+    arrived("OY2a")
     share_other(3)
-    arrived("OX2")
+    arrived("OX2a")
     share_other(7)
+    arrived("OY2b")
+    arrived("OX2b")
 
     @pl.when(end == 1)
     def _():

time: 77.8 us -> 76.8 us (0.987); the launches traced: 76.6 us -> 76.8 us
  no operation moved by 1% of the time
where the time goes in v5:
time: 76.8 us
  Pallas kernels  76.1 us (99%)
    pallas_call x1, Pallas kernels, body(): pl.pallas_call(kernel, out_shape=(pltpu.VMEM((256, 1024), BF16), pltpu.VM...  74.4 us
    pallas_call x1, Pallas kernels, body(): pl.pallas_call(settle, out_shape=tuple((jax.ShapeDtypeStruct(result.shape...  1.72 us

profile of v5, /device:TPU:1, one launch (start us, length us, event | category | flops | bytes accessed | tf_op | source)
XLA Modules:
  0.0 76.8 jit_solution(15138332268971567897)
XLA Ops:
  0.6 74.4 %shard_map.58 = (bf16[256,1024]{1,0:T(8,128)(2,1)S(1)}, bf16[256,1024]{1,0:T(8,128)(2,1)S(1)}, bf16[2,8,128,512]{3,2,1,0:T(8,128)(2,1)S(1)}) custom-call(bf16[256,1024]{1,0:T(8,128)(2,1)} %x_ref.1, bf16[2,8,512,512]{3,2,1,0:T(8,128)(2,1)} %w_ref.1, bf16[256,1024]{1,0:T(8,128)(2,1)} %g_ref.1), custom_call_target="tpu_custom_call" | custom-call | flops 6442450944 | bytes 12582912 | tf_op jit(solution)/shard_map/pallas_call | solution.py:375
  75.0 1.7 %shard_map.59 = (bf16[256,1024]{1,0:T(8,128)(2,1)}, bf16[256,1024]{1,0:T(8,128)(2,1)}, bf16[2,8,128,512]{3,2,1,0:T(8,128)(2,1)}) custom-call(bf16[256,1024]{1,0:T(8,128)(2,1)S(1)} %get-tuple-element.6.out_in, bf16[256,1024]{1,0:T(8,128)(2,1)S(1)} %get-tuple-element.7.ig_in, bf16[2,8,128,512]{3,2,1,0:T(8,128)(2,1)S(1)} %get-tuple-element.8.dw_in), custom_call_target="tpu_custom_call" | custom-call | tf_op jit(solution)/shard_map/pallas_call | solution.py:406

commit v6 on v5

--- a/solution.py
+++ b/solution.py
@@ -313,14 +313,17 @@
     weight_grad(0)
     add_and_pass(1)
     weight_grad(1)
-    for s in (4, 2, 6):
-        arrived(f"C{s}")
-        arrived(f"D{s}")
-        weight_grad(s)
+    arrived("C4")
+    arrived("D4")
+    weight_grad(4)
     arrived("OY2a")
     share_other(3)
     arrived("OX2a")
     share_other(7)
+    for s in (2, 6):
+        arrived(f"C{s}")
+        arrived(f"D{s}")
+        weight_grad(s)
     arrived("OY2b")
     arrived("OX2b")
 

time: 76.8 us -> 75.8 us (0.987)
  Pallas kernels: 76.1 us -> 75.1 us
    pallas_call x1, Pallas kernels: 74.4 us -> 73.4 us  [body(): pl.pallas_call(kernel, out_shape=(pltpu.VMEM((256, 1024), BF16), pltpu.VM...]
where the time goes in v6:
time: 75.8 us; the launch traced here: 75.7 us
  Pallas kernels  75.1 us (99%)
    pallas_call x1, Pallas kernels, body(): pl.pallas_call(kernel, out_shape=(pltpu.VMEM((256, 1024), BF16), pltpu.VM...  73.4 us
    pallas_call x1, Pallas kernels, body(): pl.pallas_call(settle, out_shape=tuple((jax.ShapeDtypeStruct(result.shape...  1.72 us

profile of v6, /device:TPU:1, one launch (start us, length us, event | category | flops | bytes accessed | tf_op | source)
XLA Modules:
  0.0 75.7 jit_solution(11470539931644835920)
XLA Ops:
  0.6 73.4 %shard_map.58 = (bf16[256,1024]{1,0:T(8,128)(2,1)S(1)}, bf16[256,1024]{1,0:T(8,128)(2,1)S(1)}, bf16[2,8,128,512]{3,2,1,0:T(8,128)(2,1)S(1)}) custom-call(bf16[256,1024]{1,0:T(8,128)(2,1)} %x_ref.1, bf16[2,8,512,512]{3,2,1,0:T(8,128)(2,1)} %w_ref.1, bf16[256,1024]{1,0:T(8,128)(2,1)} %g_ref.1), custom_call_target="tpu_custom_call" | custom-call | flops 6442450944 | bytes 12582912 | tf_op jit(solution)/shard_map/pallas_call | solution.py:378
  74.0 1.7 %shard_map.59 = (bf16[256,1024]{1,0:T(8,128)(2,1)}, bf16[256,1024]{1,0:T(8,128)(2,1)}, bf16[2,8,128,512]{3,2,1,0:T(8,128)(2,1)}) custom-call(bf16[256,1024]{1,0:T(8,128)(2,1)S(1)} %get-tuple-element.6.out_in, bf16[256,1024]{1,0:T(8,128)(2,1)S(1)} %get-tuple-element.7.ig_in, bf16[2,8,128,512]{3,2,1,0:T(8,128)(2,1)S(1)} %get-tuple-element.8.dw_in), custom_call_target="tpu_custom_call" | custom-call | tf_op jit(solution)/shard_map/pallas_call | solution.py:409
